TPU v7x, 32 devices: a whole 2x2x4 slice. The times are simulated.
32 devices in a mesh: nodes: 8 (over z, x), feat: 4 (over y, core).
Axes of the slice: x: 2, y: 2, z: 4, core: 2. Of those that a mesh axis runs over, the one named last changes fastest.
Arguments:
- features: bfloat16 [7680, 8, 602], P('nodes', 'feat'), may hold values from -6 to 6
- adjacency: int32 [7680, 8, 7680], P('nodes', 'feat'), may hold values from 0 to 2, as said below
- alpha_hits: int32 [7680, 8], P('nodes', 'feat'), may hold values from 1 to 5
- lambda_hits: int32 [7680, 8], P('nodes', 'feat'), may hold values from 1 to 5
- train_mask: int32 [7680, 8], P('nodes', 'feat'), may hold values from 0 to 1, as said below
- labels: int32 [7680, 8], P('nodes', 'feat'), may hold values from 0 to 40
- w_in: float32 [602, 512], P(None, 'feat'), may hold values from -0.25 to 0.25
- w_pair: float32 [3, 512, 1024], P(None, None, 'feat'), may hold values from -0.25 to 0.25
- w_proj: float32 [3, 1024, 512], P(None, None, 'feat'), may hold values from -0.1875 to 0.1875
- w_head: float32 [512, 41], P('feat'), may hold values from -0.5 to 0.5
- m_in: float32 [602, 512], P(None, 'feat'), may hold values from -0.00061035156 to 0.00061035156
- m_pair: float32 [3, 512, 1024], P(None, None, 'feat'), may hold values from -0.00061035156 to 0.00061035156
- m_proj: float32 [3, 1024, 512], P(None, None, 'feat'), may hold values from -0.00061035156 to 0.00061035156
- m_head: float32 [512, 41], P('feat'), may hold values from -0.0012207031 to 0.0012207031
- v_in: float32 [602, 512], P(None, 'feat'), may hold values from 1.6276042e-10 to 6.5104167e-10
- v_pair: float32 [3, 512, 1024], P(None, None, 'feat'), may hold values from 1.6276042e-10 to 6.5104167e-10
- v_proj: float32 [3, 1024, 512], P(None, None, 'feat'), may hold values from 1.6276042e-10 to 6.5104167e-10
- v_head: float32 [512, 41], P('feat'), may hold values from 6.5104167e-10 to 2.6041667e-09
Outputs:
- loss_sum: float32 [], replicated
- train_count: float32 [], replicated
- new_m_in: float32 [602, 512], P(None, 'feat')
- new_v_in: float32 [602, 512], P(None, 'feat')
- new_w_in: float32 [602, 512], P(None, 'feat')
- new_m_pair: float32 [3, 512, 1024], P(None, None, 'feat')
- new_v_pair: float32 [3, 512, 1024], P(None, None, 'feat')
- new_w_pair: float32 [3, 512, 1024], P(None, None, 'feat')
- new_m_proj: float32 [3, 1024, 512], P(None, None, 'feat')
- new_v_proj: float32 [3, 1024, 512], P(None, None, 'feat')
- new_w_proj: float32 [3, 1024, 512], P(None, None, 'feat')
- new_m_head: float32 [512, 41], P('feat')
- new_v_head: float32 [512, 41], P('feat')
- new_w_head: float32 [512, 41], P('feat')
Inputs may be any that keep to these rules, and one draw needn't show every extreme that they name: `adjacency`: entries are 0, 1 or 2. In each subgraph trailing nodes may be padding: their rows and columns are zero. `train_mask`: padding nodes (those with no edges at the end of a subgraph) are never training nodes.
All inputs are finite; a program needn't handle non-finite values.
Results may differ from a plain program's by a relative error of at most 0.019.
Values may be sent and summed in bfloat16 or wider, within the bound.
A program may use at most 320 MiB of HBM per device.

v0:
```python
import jax
import jax.numpy as jnp
from jax import lax
from jax.sharding import PartitionSpec as P

STEP = 5


B1 = 0.9
B2 = 0.999
ADAM_EPS = 1e-06
DECAY = 0.01
RATE = 0.5
SMOOTH = 0.1
NORM_EPS = 1e-06


def activate(z):
    act = jax.nn.silu(z)
    return act * lax.rsqrt(jnp.mean(act * act, axis=-1, keepdims=True) + NORM_EPS)


def layer_forward(hidden, pair_b, proj_b, links, inv_deg, alpha_f):
    width = proj_b.shape[1]
    hidden_b = hidden.astype(jnp.bfloat16)
    paired = jnp.einsum("rsd,dk->rsk", hidden_b, pair_b, preferred_element_type=jnp.float32)
    message = (paired[..., width:] / alpha_f).astype(jnp.bfloat16)
    gathered = jnp.einsum(
        "rsc,csd->rsd",
        links,
        lax.all_gather(message, "nodes", axis=0, tiled=True),
        preferred_element_type=jnp.float32,
    )
    joined = jnp.concatenate([paired[..., :width], gathered * inv_deg[..., None]], axis=-1).astype(
        jnp.bfloat16
    )
    z_pre = jnp.einsum("rsk,kd->rsd", joined, proj_b, preferred_element_type=jnp.float32)
    return (activate(z_pre), (hidden_b, joined, z_pre))


def layer_backward(grad_h, kept, pair_b, proj_b, links, inv_deg, alpha_f):
    hidden_b, joined, z_pre = kept
    width = proj_b.shape[1]
    _, pull = jax.vjp(activate, z_pre)
    grad_z = pull(grad_h)[0].astype(jnp.bfloat16)
    grad_proj = jnp.einsum("rsk,rsd->kd", joined, grad_z, preferred_element_type=jnp.float32)
    grad_joined = jnp.einsum("rsd,kd->rsk", grad_z, proj_b, preferred_element_type=jnp.float32)
    grad_gathered = (grad_joined[..., width:] * inv_deg[..., None]).astype(jnp.bfloat16)
    grad_message = lax.psum_scatter(
        jnp.einsum("rsc,rsd->csd", links, grad_gathered, preferred_element_type=jnp.float32).astype(
            jnp.bfloat16
        ),
        "nodes",
        scatter_dimension=0,
        tiled=True,
    ).astype(jnp.float32)
    grad_paired = jnp.concatenate(
        [grad_joined[..., :width], grad_message / alpha_f], axis=-1
    ).astype(jnp.bfloat16)
    grad_pair = jnp.einsum("rsd,rsk->dk", hidden_b, grad_paired, preferred_element_type=jnp.float32)
    grad_hidden = jnp.einsum("rsk,dk->rsd", grad_paired, pair_b, preferred_element_type=jnp.float32)
    return (grad_hidden, grad_pair, grad_proj)


def lamb_parts(weight, grad, first, second):
    first_new = B1 * first + (1.0 - B1) * grad
    second_new = B2 * second + (1.0 - B2) * grad * grad
    update = (
        first_new / (1.0 - B1**STEP) / (jnp.sqrt(second_new / (1.0 - B2**STEP)) + ADAM_EPS)
        + DECAY * weight
    )
    return (first_new, second_new, update)


def body(
    features,
    adjacency,
    alpha_hits,
    lambda_hits,
    train_mask,
    labels,
    w_in,
    w_pair,
    w_proj,
    w_head,
    m_in,
    m_pair,
    m_proj,
    m_head,
    v_in,
    v_pair,
    v_proj,
    v_head,
):
    full_in, full_pair, full_proj, full_head = (
        lax.all_gather(w_in.astype(jnp.bfloat16), "feat", axis=1, tiled=True),
        lax.all_gather(w_pair.astype(jnp.bfloat16), "feat", axis=2, tiled=True),
        lax.all_gather(w_proj.astype(jnp.bfloat16), "feat", axis=2, tiled=True),
        lax.all_gather(w_head.astype(jnp.bfloat16), "feat", axis=0, tiled=True),
    )
    layers = full_pair.shape[0]
    classes = full_head.shape[1]
    links = adjacency.astype(jnp.bfloat16)
    inv_deg = 1.0 / jnp.maximum(jnp.sum(adjacency, axis=2).astype(jnp.float32), 1.0)
    alpha_f = alpha_hits.astype(jnp.float32)[..., None]
    hidden = jnp.einsum("rsf,fd->rsd", features, full_in, preferred_element_type=jnp.float32)
    saved = []
    for layer in range(layers):
        hidden, kept = layer_forward(
            hidden, full_pair[layer], full_proj[layer], links, inv_deg, alpha_f
        )
        saved.append(kept)
    last_b = hidden.astype(jnp.bfloat16)
    logits = jnp.einsum("rsd,dc->rsc", last_b, full_head, preferred_element_type=jnp.float32)
    logp = jax.nn.log_softmax(logits, axis=-1)
    onehot = (labels[..., None] == jnp.arange(classes, dtype=jnp.int32)).astype(jnp.float32)
    target = (1.0 - SMOOTH) * onehot + SMOOTH / classes
    weight = train_mask.astype(jnp.float32) / lambda_hits.astype(jnp.float32)
    local_loss = jnp.sum(weight * -jnp.sum(target * logp, axis=-1))
    local_count = jnp.sum(train_mask.astype(jnp.float32))
    loss_sum, train_count = lax.psum((local_loss, local_count), ("nodes", "feat"))
    grad_logits = ((weight / train_count)[..., None] * (jnp.exp(logp) - target)).astype(
        jnp.bfloat16
    )
    grad_head = jnp.einsum("rsd,rsc->dc", last_b, grad_logits, preferred_element_type=jnp.float32)
    grad_h = jnp.einsum("rsc,dc->rsd", grad_logits, full_head, preferred_element_type=jnp.float32)
    pair_grads = []
    proj_grads = []
    for layer in reversed(range(layers)):
        grad_h, grad_pair, grad_proj = layer_backward(
            grad_h, saved[layer], full_pair[layer], full_proj[layer], links, inv_deg, alpha_f
        )
        pair_grads.insert(0, grad_pair)
        proj_grads.insert(0, grad_proj)
    grad_in = jnp.einsum(
        "rsf,rsd->fd", features, grad_h.astype(jnp.bfloat16), preferred_element_type=jnp.float32
    )
    partial_grads = (grad_in, jnp.stack(pair_grads), jnp.stack(proj_grads), grad_head)
    summed = (
        lax.psum(partial_grads[0].astype(jnp.bfloat16), "nodes").astype(jnp.float32),
        lax.psum(partial_grads[1].astype(jnp.bfloat16), "nodes").astype(jnp.float32),
        lax.psum(partial_grads[2].astype(jnp.bfloat16), "nodes").astype(jnp.float32),
        lax.psum(partial_grads[3].astype(jnp.bfloat16), "nodes").astype(jnp.float32),
    )
    grads = (
        lax.psum_scatter(
            summed[0].astype(jnp.bfloat16), "feat", scatter_dimension=1, tiled=True
        ).astype(jnp.float32),
        lax.psum_scatter(
            summed[1].astype(jnp.bfloat16), "feat", scatter_dimension=2, tiled=True
        ).astype(jnp.float32),
        lax.psum_scatter(
            summed[2].astype(jnp.bfloat16), "feat", scatter_dimension=2, tiled=True
        ).astype(jnp.float32),
        lax.psum_scatter(
            summed[3].astype(jnp.bfloat16), "feat", scatter_dimension=0, tiled=True
        ).astype(jnp.float32),
    )
    parts_in = lamb_parts(w_in, grads[0], m_in, v_in)
    parts_pair = lamb_parts(w_pair, grads[1], m_pair, v_pair)
    parts_proj = lamb_parts(w_proj, grads[2], m_proj, v_proj)
    parts_head = lamb_parts(w_head, grads[3], m_head, v_head)
    weight_sq = jnp.concatenate(
        [
            jnp.sum(w_in * w_in)[None],
            jnp.sum(w_pair * w_pair, axis=(1, 2)),
            jnp.sum(w_proj * w_proj, axis=(1, 2)),
            jnp.sum(w_head * w_head)[None],
        ]
    )
    update_sq = jnp.concatenate(
        [
            jnp.sum(parts_in[2] * parts_in[2])[None],
            jnp.sum(parts_pair[2] * parts_pair[2], axis=(1, 2)),
            jnp.sum(parts_proj[2] * parts_proj[2], axis=(1, 2)),
            jnp.sum(parts_head[2] * parts_head[2])[None],
        ]
    )
    norms = lax.psum(jnp.stack([weight_sq, update_sq]), "feat")
    trust = jnp.sqrt(norms[0]) / jnp.sqrt(norms[1])
    new_in = w_in - RATE * trust[0] * parts_in[2]
    new_pair = w_pair - RATE * trust[1 : 1 + layers][:, None, None] * parts_pair[2]
    new_proj = w_proj - RATE * trust[1 + layers : 1 + 2 * layers][:, None, None] * parts_proj[2]
    new_head = w_head - RATE * trust[1 + 2 * layers] * parts_head[2]
    return (
        loss_sum,
        train_count,
        parts_in[0],
        parts_in[1],
        new_in,
        parts_pair[0],
        parts_pair[1],
        new_pair,
        parts_proj[0],
        parts_proj[1],
        new_proj,
        parts_head[0],
        parts_head[1],
        new_head,
    )


def solution(mesh):
    return jax.shard_map(
        body,
        mesh=mesh,
        in_specs=(
            P("nodes", "feat", None),
            P("nodes", "feat", None),
            P("nodes", "feat"),
            P("nodes", "feat"),
            P("nodes", "feat"),
            P("nodes", "feat"),
            P(None, "feat"),
            P(None, None, "feat"),
            P(None, None, "feat"),
            P("feat", None),
            P(None, "feat"),
            P(None, None, "feat"),
            P(None, None, "feat"),
            P("feat", None),
            P(None, "feat"),
            P(None, None, "feat"),
            P(None, None, "feat"),
            P("feat", None),
        ),
        out_specs=(
            P(),
            P(),
            P(None, "feat"),
            P(None, "feat"),
            P(None, "feat"),
            P(None, None, "feat"),
            P(None, None, "feat"),
            P(None, None, "feat"),
            P(None, None, "feat"),
            P(None, None, "feat"),
            P(None, None, "feat"),
            P("feat", None),
            P("feat", None),
            P("feat", None),
        ),
        check_vma=False,
    )
```

profile of v0, /device:TPU:0, one launch (start us, length us, event | category | flops | bytes accessed | tf_op | source)
XLA Modules:
  0.0 2011.8 jit_solution(2950916331634395345)
XLA Ops:
  11.5 9.2 all_gather.21
  23.7 18.1 all-gather.6.cloned.1.call-done
  41.8 4.0 fusion.93
  52.1 50.5 %fusion.147 = (s32[960,2]{1,0:T(8,128)S(1)}, bf16[960,2,7680]{2,1,0:T(2,128)(2,1)}) fusion(s32[960,2,7680]{2,1,0:T(2,128)} %param.19), kind=kLoop, calls=%fused_computation.206 | loop fusion | flops 29489280 | bytes 88481280 | tf_op jit(solution)/shard_map/reduce_sum | solution.py:104
  105.2 160.4 %all-gather.8.cloned.1.call-done = bf16[7680,2,512]{2,0,1:T(8,128)(2,1)} async-done(((bf16[960,2,512]{2,0,1:T(8,128)(2,1)}), bf16[7680,2,512]{2,0,1:T(8,128)(2,1)}) %all-gather.8.cloned.1.call-update) | async-done | bytes 15728656 | tf_op jit(solution)/shard_map/all_gather | solution.py:31
  265.6 27.9 %fusion.28 = bf16[960,2,512]{2,0,1:T(8,128)(2,1)} fusion(bf16[7680,2,512]{2,0,1:T(8,128)(2,1)} %all-gather.8.cloned.1.call-done, bf16[960,2,7680]{2,1,0:T(2,128)(2,1)} %get-tuple-element.38, f32[960,2]{0,1:T(2,128)S(1)} %maximum_divide_fusion), kind=kOutput, calls=%fused_computation.58 | convolution fusion | flops 15101460480 | bytes 47193600 | tf_op jit(solution)/shard_map/rsc,csd->rsd/dot_general | solution.py:28
  294.9 4.6 multiply_reduce_fusion.5
  299.6 4.7 fusion.95
  312.2 212.0 %all-gather.12.cloned.1.call-done = bf16[7680,2,512]{2,0,1:T(8,128)(2,1)} async-done(((bf16[960,2,512]{2,0,1:T(8,128)(2,1)}), bf16[7680,2,512]{2,0,1:T(8,128)(2,1)}) %all-gather.12.cloned.1.call-update) | async-done | bytes 15728656 | tf_op jit(solution)/shard_map/all_gather | solution.py:31
  524.2 27.1 %fusion.27 = bf16[960,2,512]{2,0,1:T(8,128)(2,1)} fusion(bf16[7680,2,512]{2,0,1:T(8,128)(2,1)} %all-gather.12.cloned.1.call-done, bf16[960,2,7680]{2,1,0:T(2,128)(2,1)} %get-tuple-element.38, f32[960,2]{0,1:T(2,128)S(1)} %maximum_divide_fusion), kind=kOutput, calls=%fused_computation.56 | convolution fusion | flops 15101460480 | bytes 47193600 | tf_op jit(solution)/shard_map/rsc,csd->rsd/dot_general | solution.py:28
  551.3 4.6 multiply_reduce_fusion.4
  556.0 4.7 fusion.97
  565.6 5.4 all_gather.27
  574.0 204.8 %all-gather.14.cloned.1.call-done = bf16[7680,2,512]{2,0,1:T(8,128)(2,1)} async-done(((bf16[960,2,512]{2,0,1:T(8,128)(2,1)}), bf16[7680,2,512]{2,0,1:T(8,128)(2,1)}) %all-gather.14.cloned.1.call-update) | async-done | bytes 15728656 | tf_op jit(solution)/shard_map/all_gather | solution.py:31
  778.8 27.3 %fusion.26 = bf16[960,2,512]{2,0,1:T(8,128)(2,1)} fusion(bf16[7680,2,512]{2,0,1:T(8,128)(2,1)} %all-gather.14.cloned.1.call-done, bf16[960,2,7680]{2,1,0:T(2,128)(2,1)} %get-tuple-element.38, f32[960,2]{0,1:T(2,128)S(1)} %maximum_divide_fusion), kind=kOutput, calls=%fused_computation.54 | convolution fusion | flops 15101460480 | bytes 47193600 | tf_op jit(solution)/shard_map/rsc,csd->rsd/dot_general | solution.py:28
  806.1 6.5 multiply_reduce_fusion.3
  812.7 3.4 fusion.89
  817.0 38.7 %all-reduce = (f32[]{:T(128)}, f32[]{:T(128)}) all-reduce(f32[]{:T(128)} %get-tuple-element.23, f32[]{:T(128)} %get-tuple-element.22), channel_id=1, replica_groups=mesh['nodes'=8,'feat'=4] {'nodes','feat'}, use_global_device_ids=true, to_apply=%region_8.9 | all-reduce | flops 2 | bytes 16 | tf_op jit(solution)/shard_map/psum | solution.py:121
  856.3 5.1 multiply_reduce_fusion.2
  861.5 4.4 fusion.13
  867.2 6.7 fusion.98
  873.9 27.2 %convert_bitcast_fusion.2 = bf16[7680,2,512]{2,0,1:T(8,128)(2,1)} fusion(bf16[960,2,7680]{2,1,0:T(2,128)(2,1)} %get-tuple-element.38, f32[960,2,1024]{2,0,1:T(8,128)} %fusion.98, f32[960,2]{0,1:T(2,128)S(1)} %maximum_divide_fusion), kind=kOutput, calls=%fused_computation.4 | convolution fusion | flops 15109324800 | bytes 49159680 | tf_op jit(solution)/shard_map/rsc,rsd->csd/dot_general | solution.py:50
  904.0 249.6 %reduce-scatter.14.cloned.1.call-done = bf16[960,2,512]{2,0,1:T(8,128)(2,1)} async-done(((bf16[7680,2,512]{2,0,1:T(8,128)(2,1)}), bf16[960,2,512]{2,0,1:T(8,128)(2,1)}) %reduce-scatter.14.cloned.1.call-update) | async-done | bytes 1966096 | tf_op jit(solution)/shard_map/reduce_scatter | solution.py:49
  1156.3 5.0 multiply_reduce_fusion.1
  1165.0 6.7 fusion.96
  1171.7 27.2 %convert_bitcast_fusion.1 = bf16[7680,2,512]{2,0,1:T(8,128)(2,1)} fusion(bf16[960,2,7680]{2,1,0:T(2,128)(2,1)} %get-tuple-element.38, f32[960,2,1024]{2,0,1:T(8,128)} %fusion.96, f32[960,2]{0,1:T(2,128)S(1)} %maximum_divide_fusion), kind=kOutput, calls=%fused_computation.3 | convolution fusion | flops 15109324800 | bytes 49159680 | tf_op jit(solution)/shard_map/rsc,rsd->csd/dot_general | solution.py:50
  1201.6 247.8 %reduce-scatter.16.cloned.1.call-done = bf16[960,2,512]{2,0,1:T(8,128)(2,1)} async-done(((bf16[7680,2,512]{2,0,1:T(8,128)(2,1)}), bf16[960,2,512]{2,0,1:T(8,128)(2,1)}) %reduce-scatter.16.cloned.1.call-update) | async-done | bytes 1966096 | tf_op jit(solution)/shard_map/reduce_scatter | solution.py:49
  1452.1 5.0 multiply_reduce_fusion
  1460.9 6.7 fusion.94
  1467.6 27.2 %convert_bitcast_fusion = bf16[7680,2,512]{2,0,1:T(8,128)(2,1)} fusion(bf16[960,2,7680]{2,1,0:T(2,128)(2,1)} %get-tuple-element.38, f32[960,2,1024]{2,0,1:T(8,128)} %fusion.94, f32[960,2]{0,1:T(2,128)S(1)} %maximum_divide_fusion), kind=kOutput, calls=%fused_computation.2 | convolution fusion | flops 15109324800 | bytes 49159680 | tf_op jit(solution)/shard_map/rsc,rsd->csd/dot_general | solution.py:50
  1496.4 4.6 fusion.78
  1507.3 5.6 copy.72
  1513.0 5.8 copy.76
  1519.2 5.2 fusion.75
  1524.4 3.6 slice.180
  1528.1 217.3 %reduce-scatter.18.cloned.1.call-done = bf16[960,2,512]{2,0,1:T(8,128)(2,1)} async-done(((bf16[7680,2,512]{2,0,1:T(8,128)(2,1)}), bf16[960,2,512]{2,0,1:T(8,128)(2,1)}) %reduce-scatter.18.cloned.1.call-update) | async-done | bytes 1966096 | tf_op jit(solution)/shard_map/reduce_scatter | solution.py:49
  1748.7 7.7 fusion.84
  1758.7 5.3 fusion.74
  1768.7 3.7 fusion.92
  1773.3 11.7 reduce-scatter.24.cloned.1.call-done
  1789.2 21.3 %reduce-scatter.22.cloned.1.call-done = bf16[128,602]{1,0:T(8,128)(2,1)} async-done(((bf16[512,602]{1,0:T(8,128)(2,1)}), bf16[128,602]{1,0:T(8,128)(2,1)}) %reduce-scatter.22.cloned.1.call-update) | async-done | bytes 154128
  1812.3 39.0 %reduce-scatter.20.cloned.1.call-done = bf16[3,512,256]{2,1,0:T(8,128)(2,1)} async-done(((bf16[3,512,1024]{2,1,0:T(8,128)(2,1)}), bf16[3,512,256]{2,1,0:T(8,128)(2,1)}) %reduce-scatter.20.cloned.1.call-update) | async-done | bytes 786448 | tf_op jit(solution)/shard_map/reduce_scatter | solution.py:149
  1851.3 22.4 %reduce-scatter.26.cloned.1.call-done = bf16[128,41]{1,0:T(8,128)(2,1)} async-done(((bf16[512,41]{1,0:T(8,128)(2,1)}), bf16[128,41]{1,0:T(8,128)(2,1)}) %reduce-scatter.26.cloned.1.call-update) | async-done | bytes 10512
  1874.6 38.2 %psum.59 = bf16[128,41]{0,1:T(8,128)(2,1)S(1)} all-reduce(bf16[128,41]{0,1:T(8,128)(2,1)S(1)} %copy.75), channel_id=1, replica_groups=mesh['nodes'=8,'feat'=4] {'nodes'}, use_global_device_ids=true, to_apply=%region_30.31 | all-reduce | flops 5248 | bytes 20992 | tf_op jit(solution)/shard_map/psum | solution.py:143
  1913.4 60.2 %all-reduce.4.cloned.1.call-done = (bf16[602,128]{1,0:T(8,128)(2,1)}, bf16[3,1024,128]{2,1,0:T(8,128)(2,1)}, bf16[3,512,256]{2,1,0:T(8,128)(2,1)}) async-done(((bf16[602,128]{1,0:T(8,128)(2,1)}, bf16[3,1024,128]{2,1,0:T(8,128)(2,1)}, bf16[3,512,256]{2,1,0:T(8,128)(2,1)}), (bf16[602,128]{1,0:T(8,128)(2,1)}, bf16[3,1024,128]{2,1,0:T(8,128)(2,1)}, bf16[3,512,256]{2,1,0:T(8,128)(2,1)})) %all-reduce.4.cloned.1.call-update) | async-done | bytes 1726992 | tf_op jit(solution)/shard_map/psum | solution.py:140
  1976.4 5.3 multiply_reduce_fusion.8
  1987.5 6.8 psum.55
  1999.2 3.8 multiply_subtract_fusion
  (197 shorter events, 94.8 us)
Async XLA Ops:
  7.2 13.5 copy-start.52
  7.2 34.6 %all-gather.6.cloned.1.call-start = ((), (), s32[]{:S(2)}) async-start(), calls=%async_computation.7 | async-start | bytes 3932160 | tf_op jit(solution)/shard_map/all_gather | solution.py:97
  9.8 255.9 %all-gather.8.cloned.1.call-start = ((), (), s32[]{:S(2)}) async-start(), calls=%async_computation.8 | async-start | bytes 17694720 | tf_op jit(solution)/shard_map/all_gather | solution.py:31
  50.7 244.2 %all-gather.10.cloned.1.call-start = ((), (), s32[]{:S(2)}) async-start(), calls=%async_computation.9 | async-start | bytes 3932160 | tf_op jit(solution)/shard_map/all_gather | solution.py:98
  51.7 472.4 %all-gather.12.cloned.1.call-start = ((), (), s32[]{:S(2)}) async-start(), calls=%async_computation.10 | async-start | bytes 17694720 | tf_op jit(solution)/shard_map/all_gather | solution.py:31
  105.2 189.7 %copy-start.19 = (bf16[960,2,512]{2,0,1:T(8,128)(2,1)}, bf16[960,2,512]{2,0,1:T(8,128)(2,1)S(1)}, u32[]{:S(2)}) copy-start(bf16[960,2,512]{2,0,1:T(8,128)(2,1)S(1)} %slice.185) | copy-start | bytes 5898244
  299.6 4.8 copy-start.8
  299.6 4.8 copy-start.46
  309.2 469.6 %all-gather.14.cloned.1.call-start = ((), (), s32[]{:S(2)}) async-start(), calls=%async_computation.11 | async-start | bytes 17694720 | tf_op jit(solution)/shard_map/all_gather | solution.py:31
  312.2 239.1 %copy-start.21 = (bf16[960,2,512]{2,0,1:T(8,128)(2,1)}, bf16[960,2,512]{2,0,1:T(8,128)(2,1)S(1)}, u32[]{:S(2)}) copy-start(bf16[960,2,512]{2,0,1:T(8,128)(2,1)S(1)} %slice.184) | copy-start | bytes 5898244
  555.9 4.8 copy-start.10
  565.5 588.1 %reduce-scatter.14.cloned.1.call-start = ((), (), s32[]{:S(2)}) async-start(), calls=%async_computation.12 | async-start | bytes 17694720 | tf_op jit(solution)/shard_map/reduce_scatter | solution.py:49
  574.0 232.1 %copy-start.23 = (bf16[960,2,512]{2,0,1:T(8,128)(2,1)}, bf16[960,2,512]{2,0,1:T(8,128)(2,1)S(1)}, u32[]{:S(2)}) copy-start(bf16[960,2,512]{2,0,1:T(8,128)(2,1)S(1)} %slice.183) | copy-start | bytes 5898244
  812.7 48.8 %copy-start.42 = (f32[960,2]{0,1:T(2,128)}, f32[960,2]{0,1:T(2,128)S(1)}, u32[]{:S(2)}) copy-start(f32[960,2]{0,1:T(2,128)S(1)} %fusion.111) | copy-start | bytes 23044
  816.1 45.3 %copy-start.56 = (f32[960,2,41]{0,2,1:T(8,128)}, f32[960,2,41]{0,2,1:T(8,128)S(1)}, u32[]{:S(2)}) copy-start(f32[960,2,41]{0,2,1:T(8,128)S(1)} %fusion.89) | copy-start | bytes 944644
  856.3 5.2 copy-start.50
  901.2 548.2 %reduce-scatter.16.cloned.1.call-start = ((), (), s32[]{:S(2)}) async-start(), calls=%async_computation.13 | async-start | bytes 17694720 | tf_op jit(solution)/shard_map/reduce_scatter | solution.py:49
  904.0 257.3 %copy-start.24 = (bf16[960,2,512]{2,0,1:T(8,128)(2,1)}, bf16[960,2,512]{2,0,1:T(8,128)(2,1)S(1)}, u32[]{:S(2)}) copy-start(bf16[960,2,512]{2,0,1:T(8,128)(2,1)S(1)} %slice.182) | copy-start | bytes 5898244
  1156.3 5.0 copy-start.28
  1199.0 546.3 %reduce-scatter.18.cloned.1.call-start = ((), (), s32[]{:S(2)}) async-start(), calls=%async_computation.14 | async-start | bytes 17694720 | tf_op jit(solution)/shard_map/reduce_scatter | solution.py:49
  1201.6 255.5 %copy-start.26 = (bf16[960,2,512]{2,0,1:T(8,128)(2,1)}, bf16[960,2,512]{2,0,1:T(8,128)(2,1)S(1)}, u32[]{:S(2)}) copy-start(bf16[960,2,512]{2,0,1:T(8,128)(2,1)S(1)} %slice.181) | copy-start | bytes 5898244
  1452.1 5.0 copy-start.29
  1452.1 5.0 copy-start.47
  1452.1 5.1 copy-start.41
  1494.9 290.1 %reduce-scatter.24.cloned.1.call-start = ((), (), s32[]{:S(2)}) async-start(), calls=%async_computation.17 | async-start | bytes 3932160
  1513.0 6.2 copy-start.25
  1518.7 291.8 %reduce-scatter.22.cloned.1.call-start = ((), (), s32[]{:S(2)}) async-start(), calls=%async_computation.16 | async-start | bytes 819200
  1748.7 10.0 copy-start.27
  1758.6 92.7 %reduce-scatter.20.cloned.1.call-start = ((), (), s32[]{:S(2)}) async-start(), calls=%async_computation.15 | async-start | bytes 3932160 | tf_op jit(solution)/shard_map/reduce_scatter | solution.py:149
  1758.6 5.4 copy-start.30
  1758.6 5.4 copy-start.31
  1758.6 5.4 copy-start.55
  1768.4 105.3 %reduce-scatter.26.cloned.1.call-start = ((), (), s32[]{:S(2)}) async-start(), calls=%async_computation.18 | async-start | bytes 163840
  1772.4 140.4 %copy-start.37 = (f32[128,41]{0,1:T(8,128)S(1)}, f32[128,41]{0,1:T(8,128)}, u32[]{:S(2)}) copy-start(f32[128,41]{0,1:T(8,128)} %param.27) | copy-start | bytes 62980
  1772.4 140.4 %copy-start.48 = (f32[128,41]{0,1:T(8,128)S(1)}, f32[128,41]{0,1:T(8,128)}, u32[]{:S(2)}) copy-start(f32[128,41]{0,1:T(8,128)} %param.31) | copy-start | bytes 62980
  1772.4 140.4 %copy-start.49 = (f32[128,41]{0,1:T(8,128)S(1)}, f32[128,41]{0,1:T(8,128)}, u32[]{:S(2)}) copy-start(f32[128,41]{0,1:T(8,128)} %param.35) | copy-start | bytes 62980
  1772.4 201.3 %copy-start.12 = (f32[602,128]{1,0:T(8,128)S(1)}, f32[602,128]{1,0:T(8,128)}, u32[]{:S(2)}) copy-start(f32[602,128]{1,0:T(8,128)} %param.24) | copy-start | bytes 924676
  1772.4 201.3 %copy-start.35 = (f32[602,128]{1,0:T(8,128)S(1)}, f32[602,128]{1,0:T(8,128)}, u32[]{:S(2)}) copy-start(f32[602,128]{1,0:T(8,128)} %param.32) | copy-start | bytes 924676
  1773.2 203.2 %copy-start.1 = (f32[3,1024,128]{2,1,0:T(8,128)S(1)}, f32[3,1024,128]{2,1,0:T(8,128)}, u32[]{:S(2)}) copy-start(f32[3,1024,128]{2,1,0:T(8,128)} %param.26) | copy-start | bytes 4718596
  1773.2 200.5 %all-reduce.4.cloned.1.call-start = ((), (), s32[]{:S(2)}) async-start(), calls=%async_computation.19 | async-start | bytes 3457024 | tf_op jit(solution)/shard_map/psum | solution.py:140
  1913.4 83.1 %copy-start.38 = (f32[128,41]{0,1:T(8,128)}, f32[128,41]{0,1:T(8,128)S(1)}, u32[]{:S(2)}) copy-start(f32[128,41]{0,1:T(8,128)S(1)} %get-tuple-element.35) | copy-start | bytes 62980
  1913.4 83.1 %copy-start.39 = (f32[128,41]{0,1:T(8,128)}, f32[128,41]{0,1:T(8,128)S(1)}, u32[]{:S(2)}) copy-start(f32[128,41]{0,1:T(8,128)S(1)} %get-tuple-element.36) | copy-start | bytes 62980
  1976.4 5.3 copy-start.2
  1976.4 5.3 copy-start.32
  1976.4 5.3 copy-start.33
  1976.4 5.3 copy-start.34
  1994.3 8.7 copy-start.3
  1994.3 8.7 copy-start.4
  (24 other events, 68.7 us)
Sparse Core Ops, SparseCore 0:
  10.2 31.6 all-gather.5
  50.8 214.7 all-gather.7
  267.8 27.1 all-gather.9
  309.3 214.8 all-gather.11
  565.6 213.1 all-gather.13
  901.3 252.2 reduce-scatter.13
  1199.1 250.2 reduce-scatter.15
  1495.0 250.2 reduce-scatter.17
  1747.9 37.0 reduce-scatter.23
  1788.1 22.4 reduce-scatter.21
  1813.3 37.9 reduce-scatter.19
  1854.1 19.5 reduce-scatter.25
  1879.3 94.3 all-reduce.3
where the time goes:
time: 2020 us; the launch traced here: 2010 us
  waiting for transfers between devices  1470 us (73%)
  matrix products  268 us (13%)
  other arithmetic  104 us (5%)
  blocking collectives  98.3 us (5%)
  local copies, waits for them, and re-layouts  55.1 us (3%)
    reduce_scatter x3, waiting for transfers between devices, layer_backward(): lax.psum_scatter(jnp.einsum('rsc,rsd->csd', links, grad_gathered, preferr...  715 us
    all_gather x3, waiting for transfers between devices, layer_forward(): lax.all_gather(message, 'nodes', axis=0, tiled=True)  577 us
    dot_general x3, matrix products, layer_forward(): jnp.einsum('rsc,csd->rsd', links, lax.all_gather(message, 'nodes', axis=0...  82.2 us
    dot_general x3, matrix products, layer_backward(): jnp.einsum('rsc,rsd->csd', links, grad_gathered, preferred_element_type=j...  81.7 us
    psum x1, waiting for transfers between devices, body(): lax.psum(partial_grads[0].astype(jnp.bfloat16), 'nodes').astype(jnp.float32)  60.2 us
    unnamed x16, waiting for transfers between devices  55.7 us
    reduce_sum x1, other arithmetic, body(): jnp.sum(adjacency, axis=2).astype(jnp.float32)  50.5 us
  transfers between devices with their start and end apart: 13, of which 13 were waited for; matrix products, arithmetic and copies ran while one was open for 8% of the time, Pallas kernels for 0%

commit v1 on v0

v1 whole, which is shorter than its diff:
```python
import functools
import jax
import jax.numpy as jnp
from jax import lax
from jax.experimental import pallas as pl
from jax.experimental.pallas import tpu as pltpu
from jax.sharding import PartitionSpec as P

STEP = 5


B1 = 0.9
B2 = 0.999
ADAM_EPS = 1e-06
DECAY = 0.01
RATE = 0.5
SMOOTH = 0.1
NORM_EPS = 1e-06
MESH = pl.DeviceIdType.MESH
BF = jnp.bfloat16
F32 = jnp.float32

def ag_kernel(Z,C,E,LIM,own,out,cp,rup,rdn,eup,edn,rxo,rxu,rxd,sup,sdn,seu,sed,sxo,sxu,sxd):
    R,W=own.shape; CH=R//C
    n=lax.axis_index("nodes"); f=lax.axis_index("feat")
    z=n//2; x=n%2
    dn=(n-2,f); up=(n+2,f); xn=(n+1-2*x,f)
    has_dn=z>0; has_up=z<Z-1
    bar=pltpu.get_barrier_semaphore()
    pl.semaphore_signal(bar,inc=1,device_id=xn,device_id_type=MESH)
    @pl.when(has_dn)
    def _(): pl.semaphore_signal(bar,inc=1,device_id=dn,device_id_type=MESH)
    @pl.when(has_up)
    def _(): pl.semaphore_signal(bar,inc=1,device_id=up,device_id_type=MESH)
    local=pltpu.make_async_copy(own,out.at[pl.ds(n*R,R)],cp)
    local.start()
    pl.semaphore_wait(bar,1+jnp.where(has_dn,1,0)+jnp.where(has_up,1,0))
    def rows(b,c): return pl.ds(b*R+c*CH,CH)
    def rc(b,c,s,r,dev,src=None):
        o=out.at[rows(b,c)]
        return pltpu.make_async_remote_copy(o if src is None else src,o,s,r,device_id=dev,device_id_type=MESH)
    def own_step(c,_):
        src=own.at[pl.ds(c*CH,CH)]
        rc(n,c,sxo.at[c],rxo.at[c],xn,src).start()
        pl.when(has_dn)(lambda: rc(n,c,sdn.at[0,c],rup.at[0,c],dn,src).start())
        pl.when(has_up)(lambda: rc(n,c,sup.at[0,c],rdn.at[0,c],up,src).start())
        return 0
    lax.fori_loop(0,C,own_step,0)
    H=Z-1
    for k in range(H):
        def step(c,_):
            bu=n+2*(1+k); bd=n-2*(1+k)
            not_extra = (c>=E) if k==0 else None
            @pl.when(z+1+k<=Z-1)
            def _():
                rc(bu,c,sdn.at[k,c],rup.at[k,c],dn).wait_recv()
                if k<H-1:
                    pl.when(has_dn)(lambda: rc(bu,c,sdn.at[k+1,c],rup.at[k+1,c],dn).start())
                fx=lambda: rc(bu,c,sxu.at[k,c],rxu.at[k,c],xn).start()
                fx() if k else pl.when(c>=E)(fx)
            @pl.when(z-1-k>=0)
            def _():
                rc(bd,c,sup.at[k,c],rdn.at[k,c],up).wait_recv()
                if k<H-1:
                    pl.when(has_up)(lambda: rc(bd,c,sup.at[k+1,c],rdn.at[k+1,c],up).start())
                fx=lambda: rc(bd,c,sxd.at[k,c],rxd.at[k,c],xn).start()
                fx() if k else pl.when(c>=E)(fx)
            return 0
        lax.fori_loop(0,C,step,0)
    bx=n+1-2*x
    def ex(c,_):
        rc(bx,c,sxo.at[c],rxo.at[c],xn).wait_recv()
        pl.when(has_dn)(lambda: rc(bx,c,sed.at[c],eup.at[c],dn).start())
        pl.when(has_up)(lambda: rc(bx,c,seu.at[c],edn.at[c],up).start())
        return 0
    lax.fori_loop(0,E,ex,0)
    def drain_own(c,_):
        rc(n,c,sxo.at[c],rxo.at[c],xn).wait_send()
        pl.when(c>=E)(lambda: rc(n,c,sxo.at[c],rxo.at[c],xn).wait_recv())
        pl.when(has_dn)(lambda: rc(n,c,sdn.at[0,c],rup.at[0,c],dn).wait_send())
        pl.when(has_up)(lambda: rc(n,c,sup.at[0,c],rdn.at[0,c],up).wait_send())
        return 0
    lax.fori_loop(0,C,drain_own,0)
    for k in range(H):
        def drain(c,_):
            def w(cond,sem_s,sem_r):
                pass
            @pl.when(z+1+k<=Z-1)
            def _():
                if k<H-1: pl.when(has_dn)(lambda: rc(n,c,sdn.at[k+1,c],rup.at[0,c],dn).wait_send())
                def g():
                    d=rc(n,c,sxu.at[k,c],rxu.at[k,c],xn); d.wait_send(); d.wait_recv()
                g() if k else pl.when(c>=E)(g)
                if k==0:
                    pl.when(c<E)(lambda: rc(n,c,sed.at[c],eup.at[c],dn).wait_recv())
            @pl.when(z-1-k>=0)
            def _():
                if k<H-1: pl.when(has_up)(lambda: rc(n,c,sup.at[k+1,c],rdn.at[0,c],up).wait_send())
                def g():
                    d=rc(n,c,sxd.at[k,c],rxd.at[k,c],xn); d.wait_send(); d.wait_recv()
                g() if k else pl.when(c>=E)(g)
                if k==0:
                    pl.when(c<E)(lambda: rc(n,c,seu.at[c],edn.at[c],up).wait_recv())
            return 0
        lax.fori_loop(0,C,drain,0)
    def drain_ex(c,_):
        pl.when(has_dn)(lambda: rc(bx,c,sed.at[c],eup.at[c],dn).wait_send())
        pl.when(has_up)(lambda: rc(bx,c,seu.at[c],edn.at[c],up).wait_send())
        return 0
    lax.fori_loop(0,E,drain_ex,0)
    local.wait()
def ag(a,cid,C,E,N=8,vm=False):
    R,W=a.shape; Z=N//2
    D=pltpu.SemaphoreType.DMA
    sems=[D((Z-1,C)),D((Z-1,C)),D((C,)),D((C,)),D((C,)),D((Z-1,C)),D((Z-1,C))]
    return pl.pallas_call(functools.partial(ag_kernel,Z,C,E,0),
        out_shape=jax.ShapeDtypeStruct((N*R,W),a.dtype),
        in_specs=[pl.BlockSpec(memory_space=pltpu.VMEM)],out_specs=pl.BlockSpec(memory_space=pltpu.VMEM if vm else pl.ANY),
        scratch_shapes=[D]+sems+sems,
        compiler_params=pltpu.CompilerParams(collective_id=cid,has_side_effects=True,vmem_limit_bytes=48*2**20))(a)


def activate(z):
    act = jax.nn.silu(z)
    return act * lax.rsqrt(jnp.mean(act * act, axis=-1, keepdims=True) + NORM_EPS)


def mm(a, b):
    return jnp.dot(a, b, preferred_element_type=F32)


def mm_nt(a, b):
    return lax.dot_general(a, b, (((1,), (1,)), ((), ())), preferred_element_type=F32)


def mm_tn(a, b):
    return lax.dot_general(a, b, (((0,), (0,)), ((), ())), preferred_element_type=F32)


def lamb_parts(weight, grad, first, second):
    first_new = B1 * first + (1.0 - B1) * grad
    second_new = B2 * second + (1.0 - B2) * grad * grad
    update = (
        first_new / (1.0 - B1**STEP) / (jnp.sqrt(second_new / (1.0 - B2**STEP)) + ADAM_EPS)
        + DECAY * weight
    )
    return (first_new, second_new, update)


def update(weights, firsts, seconds, grads, layers):
    w_in, w_pair, w_proj, w_head = weights
    parts = [lamb_parts(*t) for t in zip(weights, grads, firsts, seconds)]

    def squares(four):
        return jnp.concatenate(
            [
                jnp.sum(four[0] * four[0])[None],
                jnp.sum(four[1] * four[1], axis=(1, 2)),
                jnp.sum(four[2] * four[2], axis=(1, 2)),
                jnp.sum(four[3] * four[3])[None],
            ]
        )

    norms = lax.psum(jnp.stack([squares(weights), squares([p[2] for p in parts])]), "feat")
    trust = jnp.sqrt(norms[0]) / jnp.sqrt(norms[1])
    rates = [
        trust[0],
        trust[1 : 1 + layers][:, None, None],
        trust[1 + layers : 1 + 2 * layers][:, None, None],
        trust[1 + 2 * layers],
    ]
    outs = []
    for w, p, t in zip(weights, parts, rates):
        outs += [p[0], p[1], w - RATE * t * p[2]]
    return tuple(outs)


def reduce_grads(grads, dims):
    return [
        lax.psum(
            lax.psum_scatter(g.astype(BF), "feat", scatter_dimension=d, tiled=True), "nodes"
        ).astype(F32)
        for g, d in zip(grads, dims)
    ]


def body(gather, scatter, *args):
    features, adjacency, alpha_hits, lambda_hits, train_mask, labels = args[:6]
    weights, firsts, seconds = args[6:10], args[10:14], args[14:18]
    full_in, full_pair, full_proj, full_head = (
        lax.all_gather(w.astype(BF), "feat", axis=d, tiled=True)
        for w, d in zip(weights, (1, 2, 2, 0))
    )
    layers, width = full_pair.shape[0], full_pair.shape[1]
    classes = full_head.shape[1]
    subs = features.shape[1]
    ids = range(subs)
    alpha = [alpha_hits[:, s].astype(F32)[:, None] for s in ids]
    feats = [features[:, s, :] for s in ids]
    wide = -(-feats[0].shape[1] // 128) * 128 - feats[0].shape[1]
    far = [
        gather(jnp.pad((feats[s].astype(F32) / alpha[s]).astype(BF), ((0, 0), (0, wide))), s)
        for s in ids
    ]
    links = [adjacency[:, s, :].astype(BF) for s in ids]
    inv_deg = [
        1.0 / jnp.maximum(jnp.sum(adjacency[:, s, :], axis=1).astype(F32), 1.0)[:, None]
        for s in ids
    ]
    weight = train_mask.astype(F32) / lambda_hits.astype(F32)
    train_count = lax.psum(jnp.sum(train_mask.astype(F32)), ("nodes", "feat"))
    kept = [[] for _ in ids]
    near = [mm(links[s], far[s])[:, : feats[s].shape[1]].astype(BF) for s in ids]
    hidden = [mm(feats[s], full_in).astype(BF) for s in ids]
    pulled = [mm(near[s], full_in).astype(BF) for s in ids]
    for layer in range(layers):
        top, bottom = full_proj[layer][:width], full_proj[layer][width:]
        for s in ids:
            if layer == 0:
                self_v = mm(hidden[s], full_pair[0][:, :width]).astype(BF)
                agg = mm(pulled[s], full_pair[0][:, width:])
            else:
                paired = mm(hidden[s], full_pair[layer])
                self_v = paired[:, :width].astype(BF)
                message = (paired[:, width:] / alpha[s]).astype(BF)
                agg = mm(links[s], gather(message, s))
            mean_v = (agg * inv_deg[s]).astype(BF)
            z = mm(self_v, top) + mm(mean_v, bottom)
            kept[s].append((hidden[s], self_v, mean_v, z))
            hidden[s] = activate(z).astype(BF)
    loss = 0.0
    grad_in = 0.0
    grad_head = 0.0
    grad_pair = [0.0] * layers
    grad_proj = [0.0] * layers
    grad_h = []
    for s in ids:
        logits = mm(hidden[s], full_head)
        logp = jax.nn.log_softmax(logits, axis=-1)
        onehot = (labels[:, s][:, None] == jnp.arange(classes, dtype=jnp.int32)).astype(F32)
        target = (1.0 - SMOOTH) * onehot + SMOOTH / classes
        loss = loss + jnp.sum(weight[:, s] * -jnp.sum(target * logp, axis=-1))
        grad_logits = ((weight[:, s] / train_count)[:, None] * (jnp.exp(logp) - target)).astype(BF)
        grad_head = grad_head + mm_tn(hidden[s], grad_logits)
        grad_h.append(mm_nt(grad_logits, full_head))
    for layer in reversed(range(layers)):
        top, bottom = full_proj[layer][:width], full_proj[layer][width:]
        w_self, w_far = full_pair[layer][:, :width], full_pair[layer][:, width:]
        for s in ids:
            hidden_b, self_v, mean_v, z = kept[s][layer]
            _, pull = jax.vjp(activate, z)
            grad_z = pull(grad_h[s])[0].astype(BF)
            grad_proj[layer] = grad_proj[layer] + jnp.concatenate(
                [mm_tn(self_v, grad_z), mm_tn(mean_v, grad_z)]
            )
            grad_self = mm_nt(grad_z, top).astype(BF)
            grad_agg = (mm_nt(grad_z, bottom) * inv_deg[s]).astype(BF)
            if layer == 0:
                grad_pair[0] = grad_pair[0] + jnp.concatenate(
                    [mm_tn(hidden_b, grad_self), mm_tn(pulled[s], grad_agg)], axis=1
                )
                grad_in = (
                    grad_in
                    + mm_tn(feats[s], mm_nt(grad_self, w_self).astype(BF))
                    + mm_tn(near[s], mm_nt(grad_agg, w_far).astype(BF))
                )
            else:
                grad_message = scatter(mm_tn(links[s], grad_agg).astype(BF), s).astype(F32)
                grad_far = (grad_message / alpha[s]).astype(BF)
                grad_pair[layer] = grad_pair[layer] + jnp.concatenate(
                    [mm_tn(hidden_b, grad_self), mm_tn(hidden_b, grad_far)], axis=1
                )
                grad_h[s] = mm_nt(grad_self, w_self) + mm_nt(grad_far, w_far)
    loss_sum = lax.psum(loss, ("nodes", "feat"))
    grads = reduce_grads(
        [grad_in, jnp.stack(grad_pair), jnp.stack(grad_proj), grad_head], (1, 2, 2, 0)
    )
    return (loss_sum, train_count, *update(weights, firsts, seconds, grads, layers))


def solution(mesh):
    nodes = mesh.shape["nodes"]

    def gather(x, s):
        if nodes != 8:
            return lax.all_gather(x, "nodes", axis=0, tiled=True)
        return ag(x, x.shape[1] // 128, 6, 3)

    def scatter(x, s):
        return lax.psum_scatter(x, "nodes", scatter_dimension=0, tiled=True)

    row = (P("nodes", "feat", None),) * 2 + (P("nodes", "feat"),) * 4
    by_weight = (P(None, "feat"), P(None, None, "feat"), P(None, None, "feat"), P("feat", None))
    return jax.shard_map(
        functools.partial(body, gather, scatter),
        mesh=mesh,
        in_specs=row + by_weight * 3,
        out_specs=(P(), P()) + tuple(spec for spec in by_weight for _ in range(3)),
        check_vma=False,
    )
```

time: 2020 us -> 1780 us (0.88)
  waiting for transfers between devices: 1470 us -> 596 us
  Pallas kernels: 0 us -> 504 us
  other arithmetic: 104 us -> 197 us
  local copies, waits for them, and re-layouts: 55.1 us -> 92.3 us
    all_gather x5 -> x2, waiting for transfers between devices: 597 us -> 0.02 us  [body(): lax.all_gather(w.astype(BF), 'feat', axis=d, tiled=True)]
    pallas_call x0 -> x6, Pallas kernels: none -> 504 us  [ag(): pl.pallas_call(functools.partial(ag_kernel, Z, C, E, 0), out_shape=jax.Sh...]
    reduce_scatter x4 -> x5, waiting for transfers between devices: 754 us -> 505 us  [the longest x4 468 us: scatter(): return lax.psum_scatter(x, 'nodes', scatter_dimension=0, tiled=True)]
    reduce_sum x6 -> x11, other arithmetic: 62.8 us -> 130 us  [the longest x1 114 us: body(): jnp.sum(adjacency[:, s, :], axis=1).astype(F32)]
    unnamed x126 -> x332, local copies, waits for them, and re-layouts: 38.1 us -> 80.2 us
    convert_element_type x11 -> x21, other arithmetic: 19.3 us -> 47.3 us  [the longest x1 30.3 us: body(): links = [adjacency[:, s, :].astype(BF) for s in ids]]
    unnamed x16 -> x14, waiting for transfers between devices: 55.7 us -> 31.3 us
    dot_general x27 -> x84, matrix products: 265 us -> 262 us  [the longest x32 121 us: mm(): return jnp.dot(a, b, preferred_element_type=F32)]
  transfers between devices with their start and end apart: 13 -> 11, of which waited for: 13 -> 8; matrix products, arithmetic and copies ran while one was open for 8% -> 19% of each run, Pallas kernels for 0% -> 11%
where the time goes in v1:
time: 1780 us; the launch traced here: 1770 us
  waiting for transfers between devices  596 us (33%)
  Pallas kernels  504 us (28%)
  matrix products  262 us (15%)
  other arithmetic  197 us (11%)
  blocking collectives  99.7 us (6%)
  local copies, waits for them, and re-layouts  92.3 us (5%)
  between operations  18.8 us (1%)
    pallas_call x6, Pallas kernels, ag(): pl.pallas_call(functools.partial(ag_kernel, Z, C, E, 0), out_shape=jax.Sh...  504 us
    reduce_scatter x4, waiting for transfers between devices, scatter(): return lax.psum_scatter(x, 'nodes', scatter_dimension=0, tiled=True)  468 us
    dot_general x32, matrix products, mm(): return jnp.dot(a, b, preferred_element_type=F32)  121 us
    reduce_sum x1, other arithmetic, body(): jnp.sum(adjacency[:, s, :], axis=1).astype(F32)  114 us
    dot_general x34, matrix products, mm_tn(): lax.dot_general(a, b, (((0,), (0,)), ((), ())), preferred_element_type=F32)  98.1 us
    unnamed x332, local copies, waits for them, and re-layouts  80.2 us
    psum x1, waiting for transfers between devices, reduce_grads(): lax.psum(lax.psum_scatter(g.astype(BF), 'feat', scatter_dimension=d, tile...  59.7 us
    dot_general x18, matrix products, mm_nt(): lax.dot_general(a, b, (((1,), (1,)), ((), ())), preferred_element_type=F32)  43.3 us
  transfers between devices with their start and end apart: 11, of which 8 were waited for; matrix products, arithmetic and copies ran while one was open for 19% of the time, Pallas kernels for 11%

profile of v1, /device:TPU:0, one launch (start us, length us, event | category | flops | bytes accessed | tf_op | source)
XLA Modules:
  0.0 1770.3 jit_solution(1252993441852129146)
XLA Ops:
  7.2 3.6 multiply_reduce_fusion.15
  12.1 6.5 fusion.115
  20.9 99.1 %shard_map.284 = bf16[7680,640]{1,0:T(8,128)(2,1)} custom-call(bf16[960,640]{1,0:T(8,128)(2,1)S(1)} %pad.8.own), custom_call_target="tpu_custom_call" | custom-call | tf_op jit(solution)/shard_map/pallas_call | solution.py:116
  120.1 114.0 %slice_reduce_fusion = (s32[960]{0:T(1024)S(1)}, s32[960]{0:T(1024)S(1)}, s32[960,1,7680]{2,1,0:T(1,128)}, s32[960,1,7680]{2,1,0:T(1,128)}) fusion(s32[960,2,7680]{2,1,0:T(2,128)} %param.20), kind=kLoop, calls=%fused_computation.307 | loop fusion | flops 14743680 | bytes 117972480 | tf_op jit(solution)/shard_map/reduce_sum | solution.py:207
  234.1 7.8 all_gather.12
  241.8 5.2 all_gather.15
  249.0 98.9 %shard_map.281 = bf16[7680,640]{1,0:T(8,128)(2,1)} custom-call(bf16[960,640]{1,0:T(8,128)(2,1)S(1)} %pad.7.own), custom_call_target="tpu_custom_call" | custom-call | tf_op jit(solution)/shard_map/pallas_call | solution.py:116
  347.9 30.3 %fusion = (bf16[960,7680]{1,0:T(8,128)(2,1)}, bf16[960,7680]{1,0:T(8,128)(2,1)}) fusion(s32[960,1,7680]{2,1,0:T(1,128)} %get-tuple-element.80, s32[960,1,7680]{2,1,0:T(1,128)} %get-tuple-element.79), kind=kLoop, calls=%fused_computation.2 | loop fusion | flops 14745600 | bytes 88473600 | tf_op jit(solution)/shard_map/convert_element_type | solution.py:205
  378.2 17.7 fusion.46
  395.9 3.8 convolution_convert_fusion.7
  399.6 3.7 convolution_convert_fusion.9
  406.5 12.6 fusion.45
  419.1 3.2 convolution_convert_fusion.8
  422.3 3.6 slice_bitcast_fusion.1
  439.6 78.8 %shard_map.285 = bf16[7680,512]{1,0:T(8,128)(2,1)} custom-call(bf16[960,512]{1,0:T(8,128)(2,1)S(1)} %fusion.31.own), custom_call_target="tpu_custom_call" | custom-call | tf_op jit(solution)/shard_map/pallas_call | solution.py:116
  518.4 10.2 multiply_convert_fusion.9
  539.8 76.8 %shard_map.286 = bf16[7680,512]{1,0:T(8,128)(2,1)} custom-call(bf16[960,512]{1,0:T(8,128)(2,1)S(1)} %fusion.30.own), custom_call_target="tpu_custom_call" | custom-call | tf_op jit(solution)/shard_map/pallas_call | solution.py:116
  616.6 10.2 multiply_convert_fusion.7
  641.8 76.0 %shard_map.282 = bf16[7680,512]{1,0:T(8,128)(2,1)} custom-call(bf16[960,512]{1,0:T(8,128)(2,1)S(1)} %fusion.33.own), custom_call_target="tpu_custom_call" | custom-call | tf_op jit(solution)/shard_map/pallas_call | solution.py:116
  717.8 10.2 multiply_convert_fusion.15
  739.0 74.0 %shard_map.283 = bf16[7680,512]{1,0:T(8,128)(2,1)} custom-call(bf16[960,512]{1,0:T(8,128)(2,1)S(1)} %fusion.32.own), custom_call_target="tpu_custom_call" | custom-call | tf_op jit(solution)/shard_map/pallas_call | solution.py:116
  813.0 10.2 multiply_convert_fusion.13
  832.3 41.7 %all-reduce.2 = (f32[]{:T(128)}, f32[]{:T(128)}) all-reduce(f32[]{:T(128)S(6)} %add.317, f32[]{:T(128)} %get-tuple-element.90), channel_id=1, replica_groups=mesh['nodes'=8,'feat'=4] {'nodes','feat'}, use_global_device_ids=true, to_apply=%region_14.16 | all-reduce | flops 2 | bytes 16 | tf_op jit(solution)/shard_map/psum | solution.py:274
  878.6 15.1 fusion.4
  896.2 15.0 fusion.2
  917.2 116.8 %reduce-scatter.19.cloned.1.call-done = bf16[960,512]{1,0:T(8,128)(2,1)} async-done(((bf16[7680,512]{1,0:T(8,128)(2,1)}), bf16[960,512]{1,0:T(8,128)(2,1)}) %reduce-scatter.19.cloned.1.call-update) | async-done | bytes 983056 | tf_op jit(solution)/shard_map/reduce_scatter | solution.py:290
  1039.6 15.1 fusion.5
  1060.7 115.9 %reduce-scatter.15.cloned.1.call-done = bf16[960,512]{1,0:T(8,128)(2,1)} async-done(((bf16[7680,512]{1,0:T(8,128)(2,1)}), bf16[960,512]{1,0:T(8,128)(2,1)}) %reduce-scatter.15.cloned.1.call-update) | async-done | bytes 983056 | tf_op jit(solution)/shard_map/reduce_scatter | solution.py:290
  1181.2 15.0 fusion.3
  1222.0 97.1 %reduce-scatter.21.cloned.1.call-done = bf16[960,512]{1,0:T(8,128)(2,1)} async-done(((bf16[7680,512]{1,0:T(8,128)(2,1)}), bf16[960,512]{1,0:T(8,128)(2,1)}) %reduce-scatter.21.cloned.1.call-update) | async-done | bytes 983056 | tf_op jit(solution)/shard_map/reduce_scatter | solution.py:290
  1319.1 4.2 multiply_reduce_fusion
  1323.4 138.4 %reduce-scatter.17.cloned.1.call-done = bf16[960,512]{1,0:T(8,128)(2,1)} async-done(((bf16[7680,512]{1,0:T(8,128)(2,1)}), bf16[960,512]{1,0:T(8,128)(2,1)}) %reduce-scatter.17.cloned.1.call-update) | async-done | bytes 983056 | tf_op jit(solution)/shard_map/reduce_scatter | solution.py:290
  1461.8 3.6 multiply_reduce_fusion.3
  1471.0 3.7 convolution_bitcast_fusion.1
  1481.3 3.7 convolution_bitcast_fusion
  1487.2 4.8 fusion.44
  1494.7 3.3 fusion.47
  1506.4 5.7 copy.81
  1512.1 5.6 copy.91
  1546.1 15.3 reduce-scatter.27.cloned.1.call-done
  1565.7 36.4 %reduce-scatter.23.cloned.1.call-done = bf16[3,512,256]{1,2,0:T(8,128)(2,1)} async-done(((bf16[3,512,1024]{1,2,0:T(8,128)(2,1)}), bf16[3,512,256]{1,2,0:T(8,128)(2,1)}) %reduce-scatter.23.cloned.1.call-update) | async-done | bytes 786448 | tf_op jit(solution)/shard_map/reduce_scatter | solution.py:181
  1608.8 15.8 reduce-scatter.29.cloned.1.call-done
  1625.4 38.2 %psum.54 = bf16[128,41]{0,1:T(8,128)(2,1)S(1)} all-reduce(bf16[128,41]{0,1:T(8,128)(2,1)S(1)} %copy.84), channel_id=1, replica_groups=mesh['nodes'=8,'feat'=4] {'nodes'}, use_global_device_ids=true, to_apply=%region_41.43 | all-reduce | flops 5248 | bytes 20992 | tf_op jit(solution)/shard_map/psum | solution.py:180
  1664.3 59.7 %all-reduce.6.cloned.1.call-done = (bf16[602,128]{1,0:T(8,128)(2,1)}, bf16[3,1024,128]{2,1,0:T(8,128)(2,1)}, bf16[3,512,256]{1,2,0:T(8,128)(2,1)}) async-done(((bf16[602,128]{1,0:T(8,128)(2,1)}, bf16[3,1024,128]{2,1,0:T(8,128)(2,1)}, bf16[3,512,256]{1,2,0:T(8,128)(2,1)}), (bf16[602,128]{1,0:T(8,128)(2,1)}, bf16[3,1024,128]{2,1,0:T(8,128)(2,1)}, bf16[3,512,256]{1,2,0:T(8,128)(2,1)})) %all-reduce.6.cloned.1.call-update) | async-done | bytes 1726992 | tf_op jit(solution)/shard_map/psum | solution.py:180
  1724.0 5.3 multiply_reduce_fusion.14
  1736.6 6.8 psum.55
  1750.2 3.9 multiply_subtract_fusion.1
  1759.2 3.4 multiply_subtract_fusion
  (488 shorter events, 205.7 us)
Async XLA Ops:
  7.2 415.1 %all-gather.3.cloned.1.call-start = ((), (), s32[]{:S(2)}) async-start(), calls=%async_computation.8 | async-start | bytes 3932160 | tf_op jit(solution)/shard_map/all_gather | solution.py:191
  10.9 417.3 %all-gather.5.cloned.1.call-start = ((), (), s32[]{:S(2)}) async-start(), calls=%async_computation.9 | async-start | bytes 3932160 | tf_op jit(solution)/shard_map/all_gather | solution.py:191
  12.0 1022.0 %reduce-scatter.19.cloned.1.call-start = ((), (), s32[]{:S(2)}) async-start(), calls=%async_computation.12 | async-start | bytes 8847360 | tf_op jit(solution)/shard_map/reduce_scatter | solution.py:290
  120.0 114.0 %copy-start.48 = (f32[602,128]{1,0:T(8,128)S(1)}, f32[602,128]{1,0:T(8,128)}, u32[]{:S(2)}) copy-start(f32[602,128]{1,0:T(8,128)} %param.25) | copy-start | bytes 924676
  120.0 121.8 %copy-start.87 = (f32[128,41]{0,1:T(8,128)S(1)}, f32[128,41]{0,1:T(8,128)}, u32[]{:S(2)}) copy-start(f32[128,41]{0,1:T(8,128)} %param.28) | copy-start | bytes 62980
  120.0 127.0 %copy-start.120 = (s32[960,2]{0,1:T(2,128)S(1)}, s32[960,2]{0,1:T(2,128)}, u32[]{:S(2)}) copy-start(s32[960,2]{0,1:T(2,128)} %param.24) | copy-start | bytes 23044
  120.0 127.6 %copy-start.117 = (s32[960,2]{0,1:T(2,128)S(1)}, s32[960,2]{0,1:T(2,128)}, u32[]{:S(2)}) copy-start(s32[960,2]{0,1:T(2,128)} %param.23) | copy-start | bytes 23044
  120.0 127.6 %copy-start.118 = (s32[960,2]{0,1:T(2,128)S(1)}, s32[960,2]{0,1:T(2,128)}, u32[]{:S(2)}) copy-start(s32[960,2]{0,1:T(2,128)} %param.22) | copy-start | bytes 23044
  248.3 99.6 %copy-start.92 = (f32[960,2]{0,1:T(2,128)}, f32[960,2]{0,1:T(2,128)S(1)}, u32[]{:S(2)}) copy-start(f32[960,2]{0,1:T(2,128)S(1)} %get-tuple-element.91) | copy-start | bytes 23044
  378.2 28.3 %copy-start = (bf16[960,7680]{1,0:T(8,128)(2,1)S(1)}, bf16[960,7680]{1,0:T(8,128)(2,1)}, u32[]{:S(2)}) copy-start(bf16[960,7680]{1,0:T(8,128)(2,1)} %get-tuple-element.132) | copy-start | bytes 44236804
  430.2 88.1 %slice-start.4 = ((s8[14745600]{0:T(1024)(128)(4,1)}), s8[4194304]{0:T(1024)(128)(4,1)S(1)}, s32[]{:S(2)}) async-start(s8[14745600]{0:T(1024)(128)(4,1)} %bitcast.276), calls=%async_computation.23 | async-start | bytes 8388608
  430.2 88.1 %slice-start.5 = ((s8[14745600]{0:T(1024)(128)(4,1)}), s8[4194304]{0:T(1024)(128)(4,1)S(1)}, s32[]{:S(2)}) async-start(s8[14745600]{0:T(1024)(128)(4,1)} %bitcast.276), calls=%async_computation.24 | async-start | bytes 8388608
  434.7 83.7 %slice-start.6 = ((s8[14745600]{0:T(1024)(128)(4,1)}), s8[4194304]{0:T(1024)(128)(4,1)S(1)}, s32[]{:S(2)}) async-start(s8[14745600]{0:T(1024)(128)(4,1)} %bitcast.276), calls=%async_computation.25 | async-start | bytes 8388608
  439.4 79.0 %slice-start.7 = ((s8[14745600]{0:T(1024)(128)(4,1)}), s8[2162688]{0:T(1024)(128)(4,1)S(1)}, s32[]{:S(2)}) async-start(s8[14745600]{0:T(1024)(128)(4,1)} %bitcast.276), calls=%async_computation.26 | async-start | bytes 4325376
  629.0 248.2 %copy-start.103 = (f32[960]{0:T(1024)}, f32[960]{0:T(1024)S(1)}, u32[]{:S(2)}) copy-start(f32[960]{0:T(1024)S(1)} %fusion.96) | copy-start | bytes 11524
  630.2 244.4 %copy-start.83 = (f32[960,41]{0,1:T(8,128)}, f32[960,41]{0,1:T(8,128)S(1)}, u32[]{:S(2)}) copy-start(f32[960,41]{0,1:T(8,128)S(1)} %get-tuple-element.117) | copy-start | bytes 472324
  630.3 244.4 %copy-start.111 = (f32[960]{0:T(1024)}, f32[960]{0:T(1024)S(1)}, u32[]{:S(2)}) copy-start(f32[960]{0:T(1024)S(1)} %get-tuple-element.116) | copy-start | bytes 11524
  631.3 243.4 %copy-start.113 = (f32[960]{0:T(1024)}, f32[960]{0:T(1024)S(1)}, u32[]{:S(2)}) copy-start(f32[960]{0:T(1024)S(1)} %log.10) | copy-start | bytes 11524
  633.7 84.1 %slice-start = ((s8[14745600]{0:T(1024)(128)(4,1)}), s8[4194304]{0:T(1024)(128)(4,1)S(1)}, s32[]{:S(2)}) async-start(s8[14745600]{0:T(1024)(128)(4,1)} %bitcast.274), calls=%async_computation.19 | async-start | bytes 8388608
  633.7 84.1 %slice-start.1 = ((s8[14745600]{0:T(1024)(128)(4,1)}), s8[4194304]{0:T(1024)(128)(4,1)S(1)}, s32[]{:S(2)}) async-start(s8[14745600]{0:T(1024)(128)(4,1)} %bitcast.274), calls=%async_computation.20 | async-start | bytes 8388608
  636.7 81.1 %slice-start.2 = ((s8[14745600]{0:T(1024)(128)(4,1)}), s8[4194304]{0:T(1024)(128)(4,1)S(1)}, s32[]{:S(2)}) async-start(s8[14745600]{0:T(1024)(128)(4,1)} %bitcast.274), calls=%async_computation.21 | async-start | bytes 8388608
  641.5 76.2 %slice-start.3 = ((s8[14745600]{0:T(1024)(128)(4,1)}), s8[2162688]{0:T(1024)(128)(4,1)S(1)}, s32[]{:S(2)}) async-start(s8[14745600]{0:T(1024)(128)(4,1)} %bitcast.274), calls=%async_computation.22 | async-start | bytes 4325376
  827.6 46.4 %copy-start.93 = (f32[960,2]{0,1:T(2,128)S(1)}, f32[960,2]{0,1:T(2,128)}, u32[]{:S(2)}) copy-start(f32[960,2]{0,1:T(2,128)} %copy-done.92) | copy-start | bytes 23044
  878.6 15.1 copy-start.38
  893.7 282.8 %reduce-scatter.15.cloned.1.call-start = ((), (), s32[]{:S(2)}) async-start(), calls=%async_computation.10 | async-start | bytes 8847360 | tf_op jit(solution)/shard_map/reduce_scatter | solution.py:290
  896.2 15.0 copy-start.41
  911.3 407.9 %reduce-scatter.21.cloned.1.call-start = ((), (), s32[]{:S(2)}) async-start(), calls=%async_computation.13 | async-start | bytes 8847360 | tf_op jit(solution)/shard_map/reduce_scatter | solution.py:290
  914.2 119.8 %copy-start.27 = (f32[960,512]{1,0:T(8,128)S(1)}, f32[960,512]{1,0:T(8,128)}, u32[]{:S(2)}) copy-start(f32[960,512]{1,0:T(8,128)} %copy-done.26) | copy-start | bytes 5898244
  1054.7 407.1 %reduce-scatter.17.cloned.1.call-start = ((), (), s32[]{:S(2)}) async-start(), calls=%async_computation.11 | async-start | bytes 8847360 | tf_op jit(solution)/shard_map/reduce_scatter | solution.py:290
  1058.6 118.0 %copy-start.29 = (f32[960,512]{1,0:T(8,128)S(1)}, f32[960,512]{1,0:T(8,128)}, u32[]{:S(2)}) copy-start(f32[960,512]{1,0:T(8,128)} %copy-done.28) | copy-start | bytes 5898244
  1181.2 29.2 %copy-start.45 = (bf16[960,512]{1,0:T(8,128)(2,1)}, bf16[960,512]{1,0:T(8,128)(2,1)S(1)}, u32[]{:S(2)}) copy-start(bf16[960,512]{1,0:T(8,128)(2,1)S(1)} %fusion.17) | copy-start | bytes 2949124
  1196.2 348.2 %reduce-scatter.25.cloned.1.call-start = ((), (), s32[]{:S(2)}) async-start(), calls=%async_computation.15 | async-start | bytes 819200
  1220.0 99.1 %copy-start.23 = (f32[960,512]{1,0:T(8,128)S(1)}, f32[960,512]{1,0:T(8,128)}, u32[]{:S(2)}) copy-start(f32[960,512]{1,0:T(8,128)} %copy-done.22) | copy-start | bytes 5898244
  1222.0 101.3 %copy-start.106 = (f32[960]{0:T(1024)S(1)}, f32[960]{0:T(1024)}, u32[]{:S(2)}) copy-start(f32[960]{0:T(1024)} %copy-done.105) | copy-start | bytes 11524
  1323.4 142.0 %copy-start.108 = (f32[960]{0:T(1024)S(1)}, f32[960]{0:T(1024)}, u32[]{:S(2)}) copy-start(f32[960]{0:T(1024)} %copy-done.107) | copy-start | bytes 11524
  1323.4 142.0 %copy-start.25 = (f32[960,512]{1,0:T(8,128)S(1)}, f32[960,512]{1,0:T(8,128)}, u32[]{:S(2)}) copy-start(f32[960,512]{1,0:T(8,128)} %copy-done.24) | copy-start | bytes 5898244
  1323.4 142.0 %copy-start.99 = (f32[960]{0:T(1024)S(1)}, f32[960]{0:T(1024)}, u32[]{:S(2)}) copy-start(f32[960]{0:T(1024)} %copy-done.98) | copy-start | bytes 11524
  1499.1 62.3 %reduce-scatter.27.cloned.1.call-start = ((), (), s32[]{:S(2)}) async-start(), calls=%async_computation.16 | async-start | bytes 3932160
  1517.8 84.3 %reduce-scatter.23.cloned.1.call-start = ((), (), s32[]{:S(2)}) async-start(), calls=%async_computation.14 | async-start | bytes 3932160 | tf_op jit(solution)/shard_map/reduce_scatter | solution.py:181
  1540.3 84.3 %reduce-scatter.29.cloned.1.call-start = ((), (), s32[]{:S(2)}) async-start(), calls=%async_computation.17 | async-start | bytes 163840
  1544.1 179.9 %all-reduce.6.cloned.1.call-start = ((), (), s32[]{:S(2)}) async-start(), calls=%async_computation.18 | async-start | bytes 3457024 | tf_op jit(solution)/shard_map/psum | solution.py:180
  1564.2 38.0 %copy-start.30 = (f32[3,512,256]{2,1,0:T(8,128)S(1)}, f32[3,512,256]{2,1,0:T(8,128)}, u32[]{:S(2)}) copy-start(f32[3,512,256]{2,1,0:T(8,128)} %param.26) | copy-start | bytes 4718596
  1605.6 58.0 %copy-start.88 = (f32[128,41]{0,1:T(8,128)S(1)}, f32[128,41]{0,1:T(8,128)}, u32[]{:S(2)}) copy-start(f32[128,41]{0,1:T(8,128)} %param.28) | copy-start | bytes 62980
  1605.6 58.0 %copy-start.101 = (f32[128,41]{0,1:T(8,128)S(1)}, f32[128,41]{0,1:T(8,128)}, u32[]{:S(2)}) copy-start(f32[128,41]{0,1:T(8,128)} %param.32) | copy-start | bytes 62980
  1605.6 58.0 %copy-start.102 = (f32[128,41]{0,1:T(8,128)S(1)}, f32[128,41]{0,1:T(8,128)}, u32[]{:S(2)}) copy-start(f32[128,41]{0,1:T(8,128)} %param.36) | copy-start | bytes 62980
  1605.6 118.4 %copy-start.2 = (f32[3,1024,128]{2,1,0:T(8,128)S(1)}, f32[3,1024,128]{2,1,0:T(8,128)}, u32[]{:S(2)}) copy-start(f32[3,1024,128]{2,1,0:T(8,128)} %param.27) | copy-start | bytes 4718596
  1664.3 94.2 %copy-start.90 = (f32[128,41]{0,1:T(8,128)}, f32[128,41]{0,1:T(8,128)S(1)}, u32[]{:S(2)}) copy-start(f32[128,41]{0,1:T(8,128)S(1)} %get-tuple-element.77) | copy-start | bytes 62980
  1664.3 94.2 %copy-start.91 = (f32[128,41]{0,1:T(8,128)}, f32[128,41]{0,1:T(8,128)S(1)}, u32[]{:S(2)}) copy-start(f32[128,41]{0,1:T(8,128)S(1)} %get-tuple-element.78) | copy-start | bytes 62980
  (122 other events, 349.9 us)
Sparse Core Ops, SparseCore 0:
  11.0 31.6 all-gather.2
  44.8 28.9 all-gather.4
  893.9 140.0 reduce-scatter.18
  1037.5 139.0 reduce-scatter.14
  1180.1 139.0 reduce-scatter.20
  1322.6 139.0 reduce-scatter.16
  1499.2 21.5 reduce-scatter.24
  1523.4 37.9 reduce-scatter.26
  1564.1 37.9 reduce-scatter.22
  1604.9 19.5 reduce-scatter.28
  1629.6 94.3 all-reduce.5
